TPU v7x, 128 devices: a whole 4x4x4 slice. The times are simulated.
128 devices in a mesh: row: 16 (over x, y_hi, core), col: 8 (over z, y_lo).
Axes of the slice: x: 4, y: 4 (y_hi: 2, y_lo: 2; y = y_hi * 2 + y_lo), z: 4, core: 2. Of those that a mesh axis runs over, the one named last changes fastest.
Arguments:
- precision: float32 [2, 8, 16, 16, 128, 128], P(None, 'col', None, 'row'), may hold values from -1 to 33, as said below
- features: bfloat16 [4096, 16, 16, 128], P('col', None, 'row'), may hold values from -0.75 to 0.75
- weights_q: int32 [4096], P('col'), may hold values from 1 to 64
Outputs:
- factored: float32 [2, 8, 16, 16, 128, 128], P(None, 'col', None, 'row')
Inputs may be any that keep to these rules, and one draw needn't show every extreme that they name: `precision`: the top 2048 rows are symmetric; the leading 1024 x 1024 block is strictly diagonally dominant with a positive diagonal.
All inputs are finite; a program needn't handle non-finite values.
Results may differ from a plain program's by a relative error of at most 0.0023.
Values may be sent and summed in bfloat16 or wider, within the bound.
No kernel may reach another device: no remote copies, remote signals or barrier semaphores. Data moves between devices by JAX's collectives and lax.ppermute only.
A program may use at most 128 MiB of HBM per device.

v0:
```python
import jax
import jax.numpy as jnp
from jax import lax
from jax.sharding import PartitionSpec as P

PW = 1024


def tile_matrix(tiles):
    col_tiles, row_tiles, side, width = tiles.shape
    return tiles.transpose(1, 2, 0, 3).reshape(row_tiles * side, col_tiles * width)


def right_solve(rows, inverse):
    return lax.dot_general(
        rows,
        inverse,
        (((1,), (1,)), ((), ())),
        precision=lax.Precision.HIGHEST,
        preferred_element_type=jnp.float32,
    )


def gram_term(local_x, source):
    return jnp.einsum("nai,nkj->kaij", local_x, source, preferred_element_type=jnp.float32)


def factor_inverse(block):
    factor = jnp.linalg.cholesky(block)
    return jax.scipy.linalg.solve_triangular(
        factor, jnp.eye(block.shape[0], dtype=jnp.float32), lower=True
    )


def body(precision, features, weights_q):
    ncol = lax.axis_size("col")
    nrow = lax.axis_size("row")
    tcw = precision.shape[0]
    tiles_rows = precision.shape[2]
    side = precision.shape[4]
    tiles_window = tcw * ncol
    window_a = tiles_window // nrow
    panel_tiles = PW // side
    panel_local = panel_tiles // ncol
    count = features.shape[0]
    local_x = features.reshape(count, tiles_rows, side)
    window = lax.all_gather(features[:, :window_a], "row", axis=2, tiled=True)
    scale = weights_q.astype(jnp.float32) / 64.0
    weighted = (scale[:, None, None] * window.reshape(count, tiles_window, side)).astype(
        jnp.bfloat16
    )
    ordered = weighted.reshape(count, tcw, ncol, side).transpose(0, 2, 1, 3)
    gram = lax.psum_scatter(
        gram_term(local_x, ordered.reshape(count, tiles_window, side)),
        "col",
        scatter_dimension=0,
        tiled=True,
    )
    summed = precision.reshape(tcw, tiles_rows, side, side) + gram
    panel_full = lax.all_gather(
        summed[:panel_local].reshape(panel_local, 1, tiles_rows, 1, side, side),
        "col",
        axis=1,
        tiled=True,
    )
    own_rows = tile_matrix(panel_full.reshape(panel_tiles, tiles_rows, side, side))
    near = lax.all_gather(panel_full[:, :, :window_a], "row", axis=3, tiled=True)
    near_rows = tile_matrix(near.reshape(panel_tiles, tiles_window, side, side))
    inverse = factor_inverse(near_rows[:PW])
    own_lower = right_solve(own_rows, inverse)
    window_lower = right_solve(near_rows, inverse)
    col_index = lax.axis_index("col")
    row_index = lax.axis_index("row")
    own_tiles = own_lower.reshape(tiles_rows, side, panel_local, ncol, side)
    mine = (
        lax.dynamic_slice_in_dim(own_tiles, col_index, 1, 3)
        .reshape(tiles_rows, side, panel_local, side)
        .transpose(2, 0, 1, 3)
    )
    partner = lax.dynamic_slice_in_dim(window_lower.reshape(tcw, ncol, side, PW), col_index, 1, 1)[
        panel_local:
    ].reshape(tcw - panel_local, side, PW)
    update = jnp.einsum(
        "aip,bjp->baij",
        own_lower.reshape(tiles_rows, side, PW),
        partner,
        precision=lax.Precision.HIGHEST,
        preferred_element_type=jnp.float32,
    )
    global_row = (
        jnp.arange(tiles_rows, dtype=jnp.int32)[:, None] * nrow + row_index
    ) * side + jnp.arange(side, dtype=jnp.int32)[None, :]
    trailing = jnp.where(
        global_row[None, :, :, None] < PW, jnp.zeros_like(update), summed[panel_local:] - update
    )
    result = jnp.concatenate([mine, trailing], 0)
    return result.reshape(tcw, 1, tiles_rows, 1, side, side)


def solution(mesh):
    in_specs = (P(None, "col", None, "row", None, None), P("col", None, "row", None), P("col"))
    out_specs = P(None, "col", None, "row", None, None)
    return jax.shard_map(body, mesh=mesh, in_specs=in_specs, out_specs=out_specs, check_vma=False)
```

profile of v0, /device:TPU:1, one launch (start us, length us, event | category | flops | bytes accessed | tf_op | source)
XLA Modules:
  0.0 1177.5 jit_solution(88538957542860284)
XLA Ops:
  9.4 78.9 %all-gather.5.cloned.1.call-done = bf16[512,1,16,128]{3,1,2,0:T(2,128)(2,1)} async-done(((bf16[512,1,1,128]{3,1,2,0:T(2,128)(2,1)}), bf16[512,1,16,128]{3,1,2,0:T(2,128)(2,1)}) %all-gather.5.cloned.1.call-update) | async-done | bytes 2097168 | tf_op jit(solution)/shard_map/all_gather | solution.py:47
  88.3 6.5 convert_element_type.34
  99.0 12.5 %convolution_bitcast_fusion = f32[16,16,128,128]{2,3,1,0:T(8,128)} fusion(bf16[512,16,128,1]{0,2,3,1:T(8,128)(2,1)} %bitcast.183, bf16[512,16,128]{2,1,0:T(8,128)(2,1)} %bitcast.184), kind=kOutput, calls=%fused_computation.2 | convolution fusion | flops 4294967296 | bytes 20971520 | tf_op jit(solution)/shard_map/nai,nkj->kaij/dot_general | solution.py:25
  114.9 320.7 %reduce-scatter.2.cloned.1.call-done = f32[2,16,128,128]{2,3,1,0:T(8,128)} async-done(((f32[16,16,128,128]{2,3,1,0:T(8,128)}), f32[2,16,128,128]{2,3,1,0:T(8,128)}) %reduce-scatter.2.cloned.1.call-update) | async-done | bytes 2097168 | tf_op jit(solution)/shard_map/reduce_scatter | solution.py:53
  440.0 169.0 %all-gather.9.cloned.1.call-done = f32[8,16,128,128]{3,2,1,0:T(8,128)} async-done(((f32[1,16,128,128]{3,2,1,0:T(8,128)}), f32[8,16,128,128]{3,2,1,0:T(8,128)}) %all-gather.9.cloned.1.call-update) | async-done | bytes 8388624 | tf_op jit(solution)/shard_map/all_gather | solution.py:60
  614.8 13.1 %copy.25 = f32[16,128,8,128]{3,2,1,0:T(8,128)} copy(f32[16,128,8,128]{3,1,0,2:T(8,128)} %bitcast.180) | data formatting | bytes 16777216 | tf_op jit(solution)/shard_map/transpose | solution.py:11
  628.0 57.5 %all-gather.7.cloned.1.call-done = f32[1,8,1,16,128,128]{5,4,2,1,0,3:T(8,128)} async-done(((f32[1,8,1,1,128,128]{5,4,2,1,0,3:T(8,128)}), f32[1,8,1,16,128,128]{5,4,2,1,0,3:T(8,128)}) %all-gather.7.cloned.1.call-update) | async-done | bytes 8388624 | tf_op jit(solution)/shard_map/all_gather | solution.py:67
  691.6 21.5 %copy.30 = f32[16,128,8,128]{3,2,1,0:T(8,128)} copy(f32[16,128,8,128]{3,1,2,0:T(8,128)S(1)} %bitcast.175) | data formatting | bytes 16777216 | tf_op jit(solution)/shard_map/transpose | solution.py:11
  713.2 5.4 copy.27
  718.5 5.1 copy.49
  723.7 5.3 copy.28
  736.0 11.7 cholesky.223
  747.7 9.8 custom-call.63
  763.9 12.1 %cholesky.244 = f32[128,128]{1,0:T(8,128)S(1)} custom-call(f32[128,128]{1,0:T(8,128)S(1)} %cholesky.584), custom_call_target="Cholesky" | custom-call | tf_op jit(solution)/shard_map/jit(cholesky)/cholesky | solution.py:29
  776.7 9.8 custom-call.64
  789.8 11.7 cholesky.468
  802.9 9.8 custom-call.65
  816.2 11.9 %cholesky.487 = f32[128,128]{1,0:T(8,128)S(1)} custom-call(f32[128,128]{1,0:T(8,128)S(1)} %cholesky.594), custom_call_target="Cholesky" | custom-call | tf_op jit(solution)/shard_map/jit(cholesky)/cholesky | solution.py:29
  829.4 9.8 custom-call.66
  842.7 11.7 cholesky.506
  855.8 10.0 custom-call.67
  869.1 11.7 cholesky.526
  882.2 9.8 custom-call.68
  894.9 12.1 %cholesky.546 = f32[128,128]{1,0:T(8,128)S(1)} custom-call(f32[128,128]{1,0:T(8,128)S(1)} %cholesky.609), custom_call_target="Cholesky" | custom-call | tf_op jit(solution)/shard_map/jit(cholesky)/cholesky | solution.py:29
  908.4 9.8 custom-call.69
  920.8 11.7 cholesky.564
  944.4 27.7 %while.1 = (s32[]{:T(128)}, f32[1024,1024]{1,0:T(8,128)}, s32[8,2]{0,1:T(2,128)S(1)}, f32[8,128,128]{2,1,0:T(8,128)}, s32[]{:T(128)}) while((s32[]{:T(128)}, f32[1024,1024]{1,0:T(8,128)}, s32[8,2]{0,1:T(2,128)S(1)}, f32[8,128,128]{2,1,0:T(8,128)}, s32[]{:T(128)}) %tuple.57), condition=%wide.while_cond, body=%wide.while_body.sunk | while | flops 2 | bytes 132705 | solution.py:30
  972.1 79.6 %custom-call.70 = f32[8,128,128]{1,2,0:T(8,128)S(1)} custom-call(f32[8,128,128]{2,1,0:T(8,128)} %get-tuple-element.12), custom_call_target="InvertDiagBlocksLowerTriangular" | custom-call | tf_op jit(solution)/shard_map/jit(_solve_triangular)/triangular_solve | solution.py:30
  1076.0 9.3 dot_general.18
  1086.7 32.9 %fusion.3 = f32[2,8,128,1024]{3,2,1,0:T(8,128)} fusion(f32[2,8,128,1024]{3,2,1,0:T(8,128)} %dot_general.18, f32[1024,1024]{1,0:T(8,128)} %convolution_dynamic-update-slice_fusion), kind=kOutput, calls=%fused_computation.8 | convolution fusion | flops 25769803776 | bytes 20971520 | tf_op jit(solution)/shard_map/dot_general | solution.py:15
  1119.6 31.2 %fusion = f32[2048,1024]{1,0:T(8,128)S(1)} fusion(f32[1024,1024]{1,0:T(8,128)S(1)} %copy-done.7, f32[256,8,8,128]{3,2,1,0:T(8,128)} %bitcast.181), kind=kOutput, calls=%fused_computation.3 | convolution fusion | flops 25769803776 | bytes 20971520 | tf_op jit(solution)/shard_map/dot_general | solution.py:15
  1157.4 11.4 fusion.24
  (124 shorter events, 135.2 us)
Async XLA Ops:
  6.5 81.7 %all-gather.5.cloned.1.call-start = ((), (), s32[]{:S(2)}) async-start(), calls=%async_computation.1 | async-start | bytes 4456448 | tf_op jit(solution)/shard_map/all_gather | solution.py:47
  8.6 427.0 %reduce-scatter.2.cloned.1.call-start = ((), (), s32[]{:S(2)}) async-start(), calls=%async_computation.2 | async-start | bytes 18874368 | tf_op jit(solution)/shard_map/reduce_scatter | solution.py:53
  111.5 1.6 copy-start.5
  111.5 497.5 %all-gather.9.cloned.1.call-start = ((), (), s32[]{:S(2)}) async-start(), calls=%async_computation.4 | async-start | bytes 9437184 | tf_op jit(solution)/shard_map/all_gather | solution.py:60
  439.5 245.9 %all-gather.7.cloned.1.call-start = ((), (), s32[]{:S(2)}) async-start(), calls=%async_computation.3 | async-start | bytes 8912896 | tf_op jit(solution)/shard_map/all_gather | solution.py:67
  685.5 6.2 copy-start.1
  734.0 1.9 copy-start.3
  1051.6 3.9 copy-start.2
  1070.5 2.0 copy-start.6
  1086.7 32.9 %copy-start.7 = (f32[1024,1024]{1,0:T(8,128)S(1)}, f32[1024,1024]{1,0:T(8,128)}, u32[]{:S(2)}) copy-start(f32[1024,1024]{1,0:T(8,128)} %convolution_dynamic-update-slice_fusion) | copy-start | bytes 12582916
  1150.8 3.7 copy-start
  1157.4 11.4 copy-start.4
Sparse Core Ops, SparseCore 0:
  9.6 78.6 all-gather.4
  111.7 323.9 reduce-scatter.1
  439.7 169.2 all-gather.8
  611.3 74.1 all-gather.6
where the time goes:
time: 1190 us; the launch traced here: 1180 us
  waiting for transfers between devices  626 us (53%)
  other arithmetic  277 us (23%)
  matrix products  135 us (11%)
  local copies, waits for them, and re-layouts  120 us (10%)
  between operations  18.8 us (2%)
    reduce_scatter x1, waiting for transfers between devices, body(): lax.psum_scatter(gram_term(local_x, ordered.reshape(count, tiles_window,...  321 us
    another operation x30, other arithmetic, factor_inverse(): factor = jnp.linalg.cholesky(block)  173 us
    all_gather x1, waiting for transfers between devices, body(): lax.all_gather(summed[:panel_local].reshape(panel_local, 1, tiles_rows, 1...  169 us
    another operation x3, other arithmetic, factor_inverse(): jax.scipy.linalg.solve_triangular(factor, jnp.eye(block.shape[0], dtype=j...  84.4 us
    all_gather x1, waiting for transfers between devices, body(): window = lax.all_gather(features[:, :window_a], 'row', axis=2, tiled=True)  78.9 us
    dot_general x2, matrix products, right_solve(): lax.dot_general(rows, inverse, (((1,), (1,)), ((), ())), precision=lax.Pr...  64.2 us
    all_gather x1, waiting for transfers between devices, body(): lax.all_gather(panel_full[:, :, :window_a], 'row', axis=3, tiled=True)  57.5 us
    transpose x2, local copies, waits for them, and re-layouts, tile_matrix(): tiles.transpose(1, 2, 0, 3).reshape(row_tiles * side, col_tiles * width)  34.7 us
  transfers between devices with their start and end apart: 4, of which 4 were waited for; matrix products, arithmetic and copies ran while one was open for 2% of the time, Pallas kernels for 0%

commit v1 on v0

v1 whole, which is shorter than its diff:
```python
import jax
import jax.numpy as jnp
from jax import lax
from jax.sharding import PartitionSpec as P

PW = 1024
BF = jnp.bfloat16
F32 = jnp.float32


def split2(x):
    hi = x.astype(BF)
    return hi, (x - hi.astype(F32)).astype(BF)


def nt(a, b):
    return lax.dot_general(
        a,
        b,
        (((1,), (1,)), ((), ())),
        precision=lax.Precision.HIGH,
        preferred_element_type=F32,
    )


def factor_inverse(block):
    factor = jnp.linalg.cholesky(block)
    return jax.scipy.linalg.solve_triangular(
        factor, jnp.eye(block.shape[0], dtype=F32), lower=True
    )


def body(precision, features, weights_q):
    ncol = lax.axis_size("col")
    nrow = lax.axis_size("row")
    tcw = precision.shape[0]
    ta = precision.shape[2]
    side = precision.shape[4]
    count = features.shape[0]
    pt = PW // side
    tiles = precision.reshape(tcw, ta, side, side)
    xt = features.reshape(count, ta, side).transpose(1, 2, 0)
    hi, lo = split2(tiles[0, 0])
    pack = jnp.concatenate([xt[0], hi, lo], axis=1)
    got = lax.all_gather(lax.all_gather(pack, "col"), "row")
    window = got[..., :count]
    top = got[..., count : count + side].astype(F32) + got[..., count + side :].astype(F32)
    top = top.transpose(0, 2, 1, 3).reshape(nrow * side, PW)
    scale = lax.all_gather(weights_q, "col").astype(F32) / 64.0
    window = window.transpose(0, 2, 1, 3).reshape(nrow * side, ncol * count)
    weighted = (scale.reshape(1, -1) * window).astype(BF)
    rows = lax.all_to_all(xt.reshape(ncol, -1, count), "col", 0, 0, tiled=True)
    rows = rows.transpose(1, 0, 2).reshape(-1, ncol * count)
    prior = lax.all_to_all(tiles[0].reshape(ncol, -1, side), "col", 0, 0, tiled=True)
    prior = prior.transpose(1, 0, 2).reshape(-1, PW)
    gram = lax.dot_general(rows, weighted, (((1,), (1,)), ((), ())), preferred_element_type=F32)
    near = top + lax.dot_general(
        window, weighted[:PW], (((1,), (1,)), ((), ())), preferred_element_type=F32
    )
    inverse = factor_inverse(near[:PW])
    lower = nt(gram[:, :PW] + prior, inverse)
    below = nt(near[PW:], inverse)
    rest = gram[:, PW:] - nt(lower, below)
    back = jnp.stack([lower, rest]).reshape(tcw, -1, ncol, side).transpose(2, 0, 1, 3)
    back = lax.all_to_all(back, "col", 0, 0, tiled=True)
    back = back.transpose(1, 0, 2, 3).reshape(tcw, ta, side, side)
    row_tile = jnp.arange(ta, dtype=jnp.int32) * nrow + lax.axis_index("row")
    trailing = jnp.where(row_tile[:, None, None] < pt, 0.0, tiles[1] + back[1])
    result = jnp.stack([back[0], trailing])
    return result.reshape(tcw, 1, ta, 1, side, side)


def solution(mesh):
    in_specs = (P(None, "col", None, "row", None, None), P("col", None, "row", None), P("col"))
    out_specs = P(None, "col", None, "row", None, None)
    return jax.shard_map(body, mesh=mesh, in_specs=in_specs, out_specs=out_specs, check_vma=False)
```

time: 1190 us -> 855 us (0.72)
  waiting for transfers between devices: 626 us -> 177 us
  local copies, waits for them, and re-layouts: 120 us -> 171 us
  blocking collectives: 0 us -> 49 us
  starting transfers between devices: 0.5 us -> 14 us
  other arithmetic: 277 us -> 289 us
    reduce_scatter x1 -> x0, waiting for transfers between devices: 321 us -> none  [body(): lax.psum_scatter(gram_term(local_x, ordered.reshape(count, tiles_window,...]
    all_gather x3 -> x2, waiting for transfers between devices: 305 us -> 151 us  [body(): got = lax.all_gather(lax.all_gather(pack, 'col'), 'row')]
    all_gather x0 -> x1, blocking collectives: none -> 49 us  [body(): scale = lax.all_gather(weights_q, 'col').astype(F32) / 64.0]
    convert_element_type x0 -> x1, local copies, waits for them, and re-layouts: none -> 38.5 us  [body(): weighted = (scale.reshape(1, -1) * window).astype(BF)]
    all_to_all x0 -> x3, waiting for transfers between devices: none -> 25.9 us  [the longest x1 25.9 us: body(): back = lax.all_to_all(back, 'col', 0, 0, tiled=True)]
    transpose x3, local copies, waits for them, and re-layouts: 37.4 us -> 55.9 us  [the longest x2 46.8 us: body(): window = window.transpose(0, 2, 1, 3).reshape(nrow * side, ncol * count)]
    dot_general x4 -> x5, matrix products: 88 us -> 72.1 us  [the longest x1 31.6 us: body(): lax.dot_general(window, weighted[:PW], (((1,), (1,)), ((), ())), preferre...]
    all_to_all x0 -> x3, starting transfers between devices: none -> 14 us  [the longest x1 5.15 us: body(): back = lax.all_to_all(back, 'col', 0, 0, tiled=True)]
  transfers between devices with their start and end apart: 4 -> 5, of which waited for: 4 -> 3; matrix products, arithmetic and copies ran while one was open for 2% -> 66% of each run, Pallas kernels for 0% -> 0%
where the time goes in v1:
time: 855 us; the launch traced here: 850 us
  other arithmetic  289 us (34%)
  waiting for transfers between devices  177 us (21%)
  local copies, waits for them, and re-layouts  171 us (20%)
  matrix products  131 us (15%)
  blocking collectives  49 us (6%)
  between operations  19.1 us (2%)
  starting transfers between devices  14 us (2%)
    another operation x30, other arithmetic, factor_inverse(): factor = jnp.linalg.cholesky(block)  172 us
    all_gather x2, waiting for transfers between devices, body(): got = lax.all_gather(lax.all_gather(pack, 'col'), 'row')  151 us
    another operation x3, other arithmetic, factor_inverse(): jax.scipy.linalg.solve_triangular(factor, jnp.eye(block.shape[0], dtype=F...  85.1 us
    all_gather x1, blocking collectives, body(): scale = lax.all_gather(weights_q, 'col').astype(F32) / 64.0  49 us
    transpose x2, local copies, waits for them, and re-layouts, body(): window = window.transpose(0, 2, 1, 3).reshape(nrow * side, ncol * count)  46.8 us
    convert_element_type x1, local copies, waits for them, and re-layouts, body(): weighted = (scale.reshape(1, -1) * window).astype(BF)  38.5 us
    another operation x15, matrix products, factor_inverse(): jax.scipy.linalg.solve_triangular(factor, jnp.eye(block.shape[0], dtype=F...  35.8 us
    dot_general x1, matrix products, body(): lax.dot_general(window, weighted[:PW], (((1,), (1,)), ((), ())), preferre...  31.6 us
  transfers between devices with their start and end apart: 5, of which 3 were waited for; matrix products, arithmetic and copies ran while one was open for 66% of the time, Pallas kernels for 0%

profile of v1, /device:TPU:1, one launch (start us, length us, event | category | flops | bytes accessed | tf_op | source)
XLA Modules:
  0.0 850.1 jit_solution(15482136093196824225)
XLA Ops:
  11.3 44.7 %all-gather.7.cloned.1.call-done = bf16[1024,768]{1,0:T(8,128)(2,1)} async-done(((bf16[128,768]{1,0:T(8,128)(2,1)}), bf16[1024,768]{1,0:T(8,128)(2,1)}) %all-gather.7.cloned.1.call-update) | async-done | bytes 1572880 | tf_op jit(solution)/shard_map/all_gather | solution.py:45
  63.0 49.0 %all-gather.3 = s32[8,1,512]{2,1,0:T(1,128)S(1)} all-gather(s32[1,1,512]{2,1,0:T(1,128)S(1)} %bitcast.199), channel_id=2, replica_groups=mesh['row'=16,'col'=8] {'col'}, dimensions={0}, use_global_device_ids=true | all-gather | bytes 18432 | tf_op jit(solution)/shard_map/all_gather | solution.py:49
  117.1 106.1 %all-gather.9.cloned.1.call-done = bf16[128,128,768]{2,1,0:T(8,128)(2,1)} async-done(((bf16[8,128,768]{2,1,0:T(8,128)(2,1)}), bf16[128,128,768]{2,1,0:T(8,128)(2,1)}) %all-gather.9.cloned.1.call-update) | async-done | bytes 25165840 | tf_op jit(solution)/shard_map/all_gather | solution.py:45
  223.2 8.3 slice_bitcast_fusion
  231.5 8.6 %add_bitcast_fusion = f32[16,128,8,128]{3,1,2,0:T(8,128)} fusion(bf16[16,8,128,768]{3,2,1,0:T(8,128)(2,1)} %bitcast.178), kind=kLoop, calls=%fused_computation.9 | loop fusion | flops 6291456 | bytes 16777216 | tf_op jit(solution)/shard_map/transpose | solution.py:48
  240.1 38.4 %copy.54 = bf16[16,128,8,512]{3,2,1,0:T(8,128)(2,1)S(1)} copy(bf16[16,128,8,512]{3,1,2,0:T(8,128)(2,1)S(1)} %slice_bitcast_fusion) | data formatting | bytes 33554432 | tf_op jit(solution)/shard_map/transpose | solution.py:50
  278.5 10.5 %copy.69 = bf16[256,8,8,512]{3,1,2,0:T(8,128)(2,1)} copy(bf16[256,8,8,512]{3,2,1,0:T(8,128)(2,1)S(1)} %bitcast.180) | data formatting | bytes 33554432
  289.1 9.2 %copy.53 = f32[16,128,8,128]{1,0,3,2:T(8,128)} copy(f32[16,128,8,128]{3,1,2,0:T(8,128)} %add_bitcast_fusion) | data formatting | bytes 16777216 | tf_op jit(solution)/shard_map/transpose | solution.py:48
  298.2 31.6 %bitcast_add_fusion = f32[2048,1024]{0,1:T(8,128)} fusion(f32[128,8,16,128]{3,2,1,0:T(8,128)} %bitcast.186, bf16[2048,4096]{1,0:T(8,128)(2,1)} %bitcast.183, f32[4096]{0:T(1024)S(1)} %bitcast.198), kind=kOutput, calls=%fused_computation.6 | convolution fusion | flops 17194549248 | bytes 41959424 | tf_op jit(solution)/shard_map/dot_general | solution.py:57
  346.9 11.7 %cholesky.223 = f32[128,128]{1,0:T(8,128)S(1)} custom-call(f32[128,128]{1,0:T(8,128)S(1)} %cholesky.580), custom_call_target="Cholesky" | custom-call | tf_op jit(solution)/shard_map/jit(cholesky)/cholesky | solution.py:27
  358.6 9.8 %custom-call.63 = f32[1,128,128]{1,2,0:T(8,128)S(1)} custom-call(f32[1,128,128]{2,1,0:T(8,128)S(1)} %get-tuple-element.73), custom_call_target="InvertDiagBlocksLowerTriangular" | custom-call | tf_op jit(solution)/shard_map/jit(cholesky)/cholesky | solution.py:27
  374.8 11.9 %cholesky.244 = f32[128,128]{1,0:T(8,128)S(1)} custom-call(f32[128,128]{1,0:T(8,128)S(1)} %cholesky.584), custom_call_target="Cholesky" | custom-call | tf_op jit(solution)/shard_map/jit(cholesky)/cholesky | solution.py:27
  387.4 9.8 %custom-call.64 = f32[1,128,128]{1,2,0:T(8,128)S(1)} custom-call(f32[1,128,128]{2,1,0:T(8,128)S(1)} %get-tuple-element.70), custom_call_target="InvertDiagBlocksLowerTriangular" | custom-call | tf_op jit(solution)/shard_map/jit(cholesky)/cholesky | solution.py:27
  400.5 11.7 %cholesky.468 = f32[128,128]{1,0:T(8,128)S(1)} custom-call(f32[128,128]{1,0:T(8,128)S(1)} %cholesky.589), custom_call_target="Cholesky" | custom-call | tf_op jit(solution)/shard_map/jit(cholesky)/cholesky | solution.py:27
  413.5 9.8 %custom-call.65 = f32[1,128,128]{1,2,0:T(8,128)S(1)} custom-call(f32[1,128,128]{2,1,0:T(8,128)S(1)} %get-tuple-element.67), custom_call_target="InvertDiagBlocksLowerTriangular" | custom-call | tf_op jit(solution)/shard_map/jit(cholesky)/cholesky | solution.py:27
  426.9 11.9 %cholesky.487 = f32[128,128]{1,0:T(8,128)S(1)} custom-call(f32[128,128]{1,0:T(8,128)S(1)} %cholesky.594), custom_call_target="Cholesky" | custom-call | tf_op jit(solution)/shard_map/jit(cholesky)/cholesky | solution.py:27
  440.0 9.8 %custom-call.66 = f32[1,128,128]{1,2,0:T(8,128)S(1)} custom-call(f32[1,128,128]{2,1,0:T(8,128)S(1)} %get-tuple-element.64), custom_call_target="InvertDiagBlocksLowerTriangular" | custom-call | tf_op jit(solution)/shard_map/jit(cholesky)/cholesky | solution.py:27
  453.3 11.7 %cholesky.506 = f32[128,128]{1,0:T(8,128)S(1)} custom-call(f32[128,128]{1,0:T(8,128)S(1)} %cholesky.599), custom_call_target="Cholesky" | custom-call | tf_op jit(solution)/shard_map/jit(cholesky)/cholesky | solution.py:27
  466.3 10.2 %custom-call.67 = f32[1,128,128]{1,2,0:T(8,128)S(1)} custom-call(f32[1,128,128]{2,1,0:T(8,128)S(1)} %get-tuple-element.61), custom_call_target="InvertDiagBlocksLowerTriangular" | custom-call | tf_op jit(solution)/shard_map/jit(cholesky)/cholesky | solution.py:27
  479.8 11.7 %cholesky.526 = f32[128,128]{1,0:T(8,128)S(1)} custom-call(f32[128,128]{1,0:T(8,128)S(1)} %cholesky.604), custom_call_target="Cholesky" | custom-call | tf_op jit(solution)/shard_map/jit(cholesky)/cholesky | solution.py:27
  492.8 9.8 %custom-call.68 = f32[1,128,128]{1,2,0:T(8,128)S(1)} custom-call(f32[1,128,128]{2,1,0:T(8,128)S(1)} %get-tuple-element.58), custom_call_target="InvertDiagBlocksLowerTriangular" | custom-call | tf_op jit(solution)/shard_map/jit(cholesky)/cholesky | solution.py:27
  505.7 11.9 %cholesky.546 = f32[128,128]{1,0:T(8,128)S(1)} custom-call(f32[128,128]{1,0:T(8,128)S(1)} %cholesky.609), custom_call_target="Cholesky" | custom-call | tf_op jit(solution)/shard_map/jit(cholesky)/cholesky | solution.py:27
  518.9 9.8 %custom-call.69 = f32[1,128,128]{1,2,0:T(8,128)S(1)} custom-call(f32[1,128,128]{2,1,0:T(8,128)S(1)} %get-tuple-element.55), custom_call_target="InvertDiagBlocksLowerTriangular" | custom-call | tf_op jit(solution)/shard_map/jit(cholesky)/cholesky | solution.py:27
  531.3 11.7 %cholesky.564 = f32[128,128]{1,0:T(8,128)S(1)} custom-call(f32[128,128]{1,0:T(8,128)S(1)} %convolution_subtract_fusion.12), custom_call_target="Cholesky" | custom-call | tf_op jit(solution)/shard_map/jit(cholesky)/cholesky | solution.py:27
  554.9 27.3 %while.1 = (s32[]{:T(128)}, f32[1024,1024]{1,0:T(8,128)}, s32[8,2]{0,1:T(2,128)S(1)}, f32[8,128,128]{2,1,0:T(8,128)}, s32[]{:T(128)}) while((s32[]{:T(128)}, f32[1024,1024]{1,0:T(8,128)}, s32[8,2]{0,1:T(2,128)S(1)}, f32[8,128,128]{2,1,0:T(8,128)}, s32[]{:T(128)}) %tuple.59), condition=%wide.while_cond, body=%wide.while_body.sunk | while | flops 2 | bytes 132705 | solution.py:28
  582.2 80.2 %custom-call.70 = f32[8,128,128]{1,2,0:T(8,128)} custom-call(f32[8,128,128]{2,1,0:T(8,128)} %get-tuple-element.12), custom_call_target="InvertDiagBlocksLowerTriangular" | custom-call | tf_op jit(solution)/shard_map/jit(_solve_triangular)/triangular_solve | solution.py:28
  681.8 10.1 %multiply_convert_fusion = bf16[16,128,8,512]{3,1,2,0:T(8,128)(2,1)S(1)} fusion(f32[8,512]{1,0:T(8,128)S(1)} %bitcast.197, bf16[16,8,128,768]{3,2,1,0:T(8,128)(2,1)} %bitcast.179), kind=kLoop, calls=%fused_computation.2 | loop fusion | flops 25165824 | bytes 33570816 | tf_op jit(solution)/shard_map/convert_element_type | solution.py:51
  692.0 38.5 %copy.50 = bf16[16,128,8,512]{3,2,1,0:T(8,128)(2,1)S(1)} copy(bf16[16,128,8,512]{3,1,2,0:T(8,128)(2,1)S(1)} %multiply_convert_fusion) | data formatting | bytes 33554432 | tf_op jit(solution)/shard_map/convert_element_type | solution.py:51
  730.5 10.9 %copy.67 = bf16[256,8,8,512]{3,1,2,0:T(8,128)(2,1)} copy(bf16[256,8,8,512]{3,2,1,0:T(8,128)(2,1)S(1)} %bitcast.181) | data formatting | bytes 33554432
  761.6 12.4 %convolution_bitcast_fusion = f32[256,2048]{0,1:T(8,128)} fusion(bf16[2048,4096]{1,0:T(8,128)(2,1)} %bitcast.182, bf16[256,4096]{0,1:T(8,128)(2,1)} %bitcast.12), kind=kOutput, calls=%fused_computation.17 | convolution fusion | flops 4294967296 | bytes 20971520 | tf_op jit(solution)/shard_map/dot_general | solution.py:56
  776.3 17.7 %fusion.3 = f32[1024,1024]{1,0:T(8,128)} fusion(f32[1024,1024]{1,0:T(8,128)} %convolution_dynamic-update-slice_fusion, f32[2048,1024]{0,1:T(8,128)} %bitcast_add_fusion), kind=kOutput, calls=%fused_computation.11 | convolution fusion | flops 6442450944 | bytes 12582912 | tf_op jit(solution)/shard_map/dot_general | solution.py:17
  811.4 25.9 %all-to-all-done.2 = f32[8,2,256,128]{2,3,1,0:T(8,128)S(1)} async-done(((f32[8,2,256,128]{2,3,1,0:T(8,128)}), f32[8,2,256,128]{2,3,1,0:T(8,128)S(1)}, u32[]{:S(2)}, u32[]{:S(2)}) %all-to-all-start.2) | async-done | bytes 2097184 | tf_op jit(solution)/shard_map/all_to_all | solution.py:65
  (128 shorter events, 165.5 us)
Async XLA Ops:
  6.5 49.5 %all-gather.7.cloned.1.call-start = ((), (), s32[]{:S(2)}) async-start(), calls=%async_computation.3 | async-start | bytes 1769472 | tf_op jit(solution)/shard_map/all_gather | solution.py:45
  11.2 212.0 %all-gather.9.cloned.1.call-start = ((), (), s32[]{:S(2)}) async-start(), calls=%async_computation.4 | async-start | bytes 26738688 | tf_op jit(solution)/shard_map/all_gather | solution.py:45
  58.4 4.5 copy-start.4
  58.4 4.6 copy-start.7
  58.4 698.8 %all-to-all-start = ((bf16[8,256,512]{1,2,0:T(8,128)(2,1)}), bf16[8,256,512]{1,2,0:T(8,128)(2,1)}, u32[]{:S(2)}, u32[]{:S(2)}) async-start(bf16[8,256,512]{1,2,0:T(8,128)(2,1)} %copy.51), calls=%async_computation | async-start | bytes 4194304 | tf_op jit(solution)/shard_map/all_to_all | solution.py:52
  344.8 2.0 copy-start.1
  662.4 6.4 copy-start
  677.2 1.6 copy-start.2
  730.5 10.9 %copy-start.3 = (f32[640,1024]{1,0:T(8,128)S(1)}, f32[640,1024]{1,0:T(8,128)}, u32[]{:S(2)}) copy-start(f32[640,1024]{1,0:T(8,128)} %copy-done.2) | copy-start | bytes 7864324
  730.5 10.9 %copy-start.6 = (f32[128,1024]{1,0:T(8,128)S(1)}, f32[128,1024]{1,0:T(8,128)}, u32[]{:S(2)}) copy-start(f32[128,1024]{1,0:T(8,128)} %fusion.23) | copy-start | bytes 1572868
  757.2 36.8 %all-to-all-start.1 = ((f32[8,256,128]{1,2,0:T(8,128)}), f32[8,256,128]{1,2,0:T(8,128)S(1)}, u32[]{:S(2)}, u32[]{:S(2)}) async-start(f32[8,256,128]{1,2,0:T(8,128)} %copy.52), calls=%async_computation.1 | async-start | bytes 2097152 | tf_op jit(solution)/shard_map/all_to_all | solution.py:54
  806.3 31.1 %all-to-all-start.2 = ((f32[8,2,256,128]{2,3,1,0:T(8,128)}), f32[8,2,256,128]{2,3,1,0:T(8,128)S(1)}, u32[]{:S(2)}, u32[]{:S(2)}) async-start(f32[8,2,256,128]{2,3,1,0:T(8,128)} %maximum_bitcast_fusion), calls=%async_computation.2 | async-start | bytes 4194304 | tf_op jit(solution)/shard_map/all_to_all | solution.py:65
  839.1 2.2 copy-start.5
Sparse Core Ops, SparseCore 0:
  11.3 44.6 all-gather.6
  58.4 164.7 all-gather.8

commit v2 on v1

v2 whole, which is shorter than its diff:
```python
import functools

import jax
import jax.numpy as jnp
from jax import lax
from jax.experimental import pallas as pl
from jax.experimental.pallas import tpu as pltpu
from jax.sharding import PartitionSpec as P

PW = 1024
SIDE = 128
NC = 8
NQ = 4
BF = jnp.bfloat16
F32 = jnp.float32
NN = ((1,), (0,))
NT = ((1,), (1,))
TN = ((0,), (0,))
VMEM_LIMIT = 56 << 20


def dot6(a, b, dims=NN):
    return lax.dot_general(
        a, b, (dims, ((), ())), precision=lax.Precision.HIGHEST, preferred_element_type=F32
    )


def dot1(a, b, dims=NN):
    return lax.dot_general(a, b, (dims, ((), ())), preferred_element_type=F32)


def split2(x):
    hi = x.astype(BF)
    return hi, (x - hi.astype(F32)).astype(BF)


def flat(x, y, z, core):
    return ((x * 2 + y // 2) * 2 + core) * NC + z * 2 + y % 2


def shift_pairs(kind, by):
    out = []
    for x in range(4):
        for y in range(4):
            for z in range(4):
                for core in range(2):
                    nx, ny, nz, nc = x, y, z, core
                    if kind == "x":
                        nx = (x + by) % 4
                    elif kind == "core":
                        nc = 1 - core
                    elif (kind == "first") == (core == 0):
                        ny = (y + by) % 4
                    else:
                        nz = (z + by) % 4
                    out.append((flat(x, y, z, core), flat(nx, ny, nz, nc)))
    return out


def shift(x, kind, by=1):
    return lax.ppermute(x, ("row", "col"), shift_pairs(kind, by))


def ring(u, kind):
    half = u.shape[0] // 2
    prev = shift(u, kind, 1)
    nxt = shift(u, kind, -1)
    far0 = shift(prev[:half], kind, 1)
    far1 = shift(nxt[half:], kind, -1)
    return nxt, prev, far0, far1


def gather_plane(u):
    nxt, prev, far0, far1 = ring(u, "first")
    mine = jnp.stack([u, nxt, jnp.concatenate([far0, far1]), prev])
    nxt, prev, far0, far1 = ring(mine, "second")
    pieces = [mine, nxt, far0, far1, prev]
    return pieces + [shift(p, "core") for p in pieces]


PIECES = (((0, 1, 2, 3), 0), ((0, 1, 2, 3), 1), ((0, 1), 2), ((2, 3), 2), ((0, 1, 2, 3), 3))


def copies(pos_ref, piece_refs, buf, sems, width):
    out = []
    for n, ref in enumerate(piece_refs):
        firsts, second = PIECES[n % 5]
        core = pos_ref[2] if n < 5 else 1 - pos_ref[2]
        for i, first in enumerate(firsts):
            dy = jnp.where(core == 0, first, second)
            dz = jnp.where(core == 0, second, first)
            y = lax.rem(pos_ref[0] + dy, 4)
            z = lax.rem(pos_ref[1] + dz, 4)
            c = z * 2 + lax.rem(y, 2)
            q = lax.div(y, 2) * 2 + core
            out.append(
                pltpu.make_async_copy(
                    ref.at[i, :, :, pl.ds(0, width)], buf.at[c, q], sems.at[c]
                )
            )
    return out


def wait_chunk(piece_ref, buf, sems, c, width):
    for q in range(NQ):
        pltpu.make_async_copy(
            piece_ref.at[0, :, :, pl.ds(0, width)], buf.at[c, q], sems.at[c]
        ).wait()


def weigh(scale_ref, c, x):
    return (scale_ref[pl.ds(c, 1), :] * x.astype(F32)).astype(BF)


def top_kernel(pos_ref, scale_ref, *refs):
    pieces, (out_ref, buf, g_ref, sems) = refs[:10], refs[10:]
    width = buf.shape[-1]
    count = scale_ref.shape[-1]
    for copy in copies(pos_ref, pieces, buf, sems, width):
        copy.start()
    g_ref[...] = jnp.zeros_like(g_ref)

    def chunk(c, carry):
        wait_chunk(pieces[0], buf, sems, c, width)
        x = buf[c, :, :, :, :count].reshape(PW, count)
        g_ref[...] += dot1(x, weigh(scale_ref, c, x), NT)
        return carry

    lax.fori_loop(0, NC, chunk, 0)

    def tile(i, j):
        ri, rj = ((i % 4) * 2 + i // 4) * SIDE, ((j % 4) * 2 + j // 4) * SIDE
        return g_ref[ri : ri + SIDE, rj : rj + SIDE]

    for i in range(NC):
        for j in range(i + 1):
            prior = buf[j, i % 4, i // 4, :, count : count + 2 * SIDE].astype(F32)
            s = 0.5 * (tile(i, j) + tile(j, i).T) + (prior[:, :SIDE] + prior[:, SIDE:])
            out_ref[i * SIDE : (i + 1) * SIDE, j * SIDE : (j + 1) * SIDE] = s
            if j < i:
                out_ref[j * SIDE : (j + 1) * SIDE, i * SIDE : (i + 1) * SIDE] = s.T


def top_block(pos, scale, pieces):
    width = pieces[0].shape[-1]
    return pl.pallas_call(
        top_kernel,
        out_shape=jax.ShapeDtypeStruct((PW, PW), F32),
        in_specs=[
            pl.BlockSpec(memory_space=pltpu.SMEM),
            pl.BlockSpec(memory_space=pltpu.VMEM),
        ]
        + [pl.BlockSpec(memory_space=pl.ANY)] * 10,
        out_specs=pl.BlockSpec(memory_space=pltpu.VMEM),
        scratch_shapes=[
            pltpu.VMEM((NC, NQ, 2, SIDE, width), BF),
            pltpu.VMEM((PW, PW), F32),
            pltpu.SemaphoreType.DMA((NC,)),
        ],
        compiler_params=pltpu.CompilerParams(vmem_limit_bytes=VMEM_LIMIT),
    )(pos, scale, *pieces)


def rows_kernel(pos_ref, scale_ref, rows_ref, prior_ref, *refs):
    first, second = refs[:10], refs[10:20]
    near_ref, lead_ref, rest_ref, buf0, buf1, gn, gl, gr, sem0, sem1 = refs[20:]
    count = scale_ref.shape[-1]
    width = buf1.shape[-1]
    for copy in copies(pos_ref, first, buf0, sem0, count):
        copy.start()
    for copy in copies(pos_ref, second, buf1, sem1, width):
        copy.start()
    for ref in (gn, gl, gr):
        ref[...] = jnp.zeros_like(ref)

    def chunk(c, carry):
        wait_chunk(first[0], buf0, sem0, c, count)
        wait_chunk(second[0], buf1, sem1, c, width)
        w0 = weigh(scale_ref, c, buf0[c].reshape(PW, count))
        x1 = buf1[c, :, :, :, :count].reshape(PW, count)
        rows = rows_ref[c]
        gn[...] += dot1(x1, w0, NT)
        gl[...] += dot1(rows, w0, NT)
        gr[...] += dot1(rows, weigh(scale_ref, c, x1), NT)
        return carry

    lax.fori_loop(0, NC, chunk, 0)
    for j in range(NC):
        src = ((j % 4) * 2 + j // 4) * SIDE
        cols = slice(j * SIDE, (j + 1) * SIDE)
        lead_ref[:, cols] = gl[:, src : src + SIDE] + prior_ref[j]
        rest_ref[:, cols] = gr[:, src : src + SIDE]
        for i in range(NC):
            top = ((i % 4) * 2 + i // 4) * SIDE
            prior = buf1[j, i % 4, i // 4, :, count : count + 2 * SIDE].astype(F32)
            near_ref[i * SIDE : (i + 1) * SIDE, cols] = gn[
                top : top + SIDE, src : src + SIDE
            ] + (prior[:, :SIDE] + prior[:, SIDE:])


def own_rows(pos, scale, rows, prior, first, second):
    count = scale.shape[-1]
    width = first[0].shape[-1]
    own = rows.shape[1]
    vmem = pl.BlockSpec(memory_space=pltpu.VMEM)
    return pl.pallas_call(
        rows_kernel,
        out_shape=[
            jax.ShapeDtypeStruct((PW, PW), F32),
            jax.ShapeDtypeStruct((own, PW), F32),
            jax.ShapeDtypeStruct((own, PW), F32),
        ],
        in_specs=[pl.BlockSpec(memory_space=pltpu.SMEM), vmem, vmem, vmem]
        + [pl.BlockSpec(memory_space=pl.ANY)] * 20,
        out_specs=[vmem] * 3,
        scratch_shapes=[
            pltpu.VMEM((NC, NQ, 2, SIDE, count), BF),
            pltpu.VMEM((NC, NQ, 2, SIDE, width), BF),
            pltpu.VMEM((PW, PW), F32),
            pltpu.VMEM((own, PW), F32),
            pltpu.VMEM((own, PW), F32),
            pltpu.SemaphoreType.DMA((NC,)),
            pltpu.SemaphoreType.DMA((NC,)),
        ],
        compiler_params=pltpu.CompilerParams(vmem_limit_bytes=VMEM_LIMIT),
    )(pos, scale, rows, prior, *first, *second)


def factor(groups):
    m = list(groups)
    full = m[0].shape
    lane = lax.broadcasted_iota(jnp.int32, full, 1)
    sub = lax.broadcasted_iota(jnp.int32, full, 0)
    done = []
    for p in range(len(m)):
        base = 8 * p
        inside = (lane >= base) & (lane < base + 8)
        e = [jnp.broadcast_to(m[p][:, base + j : base + j + 1], full) for j in range(8)]
        s = {
            (l, j): jnp.broadcast_to(e[j][l : l + 1, :], full) for j in range(8) for l in range(j, 8)
        }
        own = jnp.where(inside, jnp.where(lane - base == sub, 1.0, 0.0), m[p])
        w = [jnp.broadcast_to(own[l : l + 1, :], full) for l in range(8)]
        t = {}
        v = [None] * 8
        for j in range(8):
            d = s[j, j]
            r = 1.0 / d
            v[j] = w[j] * lax.rsqrt(d)
            w[j] = w[j] * r
            for l in range(j + 1, 8):
                t[j, l] = s[l, j] * r
            for l in range(8):
                if l == j:
                    continue
                w[l] = w[l] - (s[l, j] if l > j else t[l, j]) * w[j]
                if l > j:
                    for k in range(j + 1, l + 1):
                        s[l, k] = s[l, k] - s[l, j] * t[j, k]
                else:
                    for k in range(j + 1, 8):
                        t[l, k] = t[l, k] - t[l, j] * t[j, k]
        for g in range(p + 1, len(m)):
            c = [jnp.broadcast_to(m[g][:, base + j : base + j + 1], full) * w[j] for j in range(8)]
            total = ((c[0] + c[1]) + (c[2] + c[3])) + ((c[4] + c[5]) + (c[6] + c[7]))
            m[g] = jnp.where(inside, 0.0, m[g]) - total
        rows = v[0]
        for j in range(1, 8):
            rows = jnp.where(sub == j, v[j], rows)
        done.append(jnp.where(lane <= sub + base, rows, 0.0))
    return done


def inverse_kernel(s_ref, inv_ref, a_ref, m_ref, z_ref):
    order = s_ref.shape[0]
    a_ref[...] = s_ref[...]
    eye = (
        lax.broadcasted_iota(jnp.int32, (SIDE, SIDE), 0)
        == lax.broadcasted_iota(jnp.int32, (SIDE, SIDE), 1)
    ).astype(F32)
    col = lax.broadcasted_iota(jnp.int32, (SIDE, order), 1)

    def step(k, carry):
        ko = pl.multiple_of(k * SIDE, SIDE)
        here = pl.ds(ko, SIDE)
        groups = [
            a_ref[pl.ds(pl.multiple_of(ko + 8 * g, 8), 8), here] for g in range(SIDE // 8)
        ]
        for g, rows in enumerate(factor(groups)):
            m_ref[8 * g : 8 * g + 8, :] = rows
        a_ref[here, here] = eye
        linv = m_ref[...]
        v = dot6(linv, a_ref[here, :])
        inv_ref[here, :] = jnp.where(col < ko + SIDE, v, 0.0)
        z_ref[...] = dot6(linv, v, TN)

        def below(i, carry):
            rows = pl.ds(pl.multiple_of(i * SIDE, SIDE), SIDE)
            left = a_ref[rows, here]
            a_ref[rows, here] = jnp.zeros((SIDE, SIDE), F32)
            a_ref[rows, :] = a_ref[rows, :] - dot6(left, z_ref[...])
            return carry

        lax.fori_loop(k + 1, order // SIDE, below, 0)
        return carry

    lax.fori_loop(0, order // SIDE, step, 0)


def factor_inverse(block):
    order = block.shape[0]
    return pl.pallas_call(
        inverse_kernel,
        out_shape=jax.ShapeDtypeStruct((order, order), F32),
        scratch_shapes=[
            pltpu.VMEM((order, order), F32),
            pltpu.VMEM((SIDE, SIDE), F32),
            pltpu.VMEM((SIDE, order), F32),
        ],
        compiler_params=pltpu.CompilerParams(vmem_limit_bytes=VMEM_LIMIT),
    )(block)


def dot3(a, b, dims):
    return dot1(a[0], b[0], dims) + (dot1(a[0], b[1], dims) + dot1(a[1], b[0], dims))


def solve_kernel(inv_ref, near_ref, lead_ref, rest_ref, out_ref, near_s, lead_s):
    step = 2 * SIDE
    for j in range(PW // step):
        k = (j + 1) * step
        cols = slice(j * step, k)
        inv = split2(inv_ref[cols, :k])
        for src, dst in ((near_ref, near_s), (lead_ref, lead_s)):
            hi, lo = split2(dot3(split2(src[:, :k]), inv, NT))
            dst[0, :, cols] = hi
            dst[1, :, cols] = lo
    for j in range(NC):
        cols = slice(j * SIDE, (j + 1) * SIDE)
        out_ref[j, 0] = lead_s[0, :, cols]
    for j in range(PW // step):
        cols = slice(j * step, (j + 1) * step)
        update = dot3((lead_s[0], lead_s[1]), (near_s[0, cols, :], near_s[1, cols, :]), NT)
        rest = (rest_ref[:, cols] - update).astype(BF)
        out_ref[2 * j, 1] = rest[:, :SIDE]
        out_ref[2 * j + 1, 1] = rest[:, SIDE:]


def solve_rows(inverse, near, lead, rest):
    own = lead.shape[0]
    return pl.pallas_call(
        solve_kernel,
        out_shape=jax.ShapeDtypeStruct((NC, 2, own, SIDE), BF),
        scratch_shapes=[pltpu.VMEM((2, PW, PW), BF), pltpu.VMEM((2, own, PW), BF)],
        compiler_params=pltpu.CompilerParams(vmem_limit_bytes=VMEM_LIMIT),
    )(inverse, near, lead, rest)


def body(precision, features, weights_q):
    tcw, ta = precision.shape[0], precision.shape[2]
    count = features.shape[0]
    row, col = lax.axis_index("row"), lax.axis_index("col")
    place = jnp.stack([(row // 2) % 2 * 2 + col % 2, col // 2, row % 2]).astype(jnp.int32)
    tiles = precision.reshape(tcw, ta, SIDE, SIDE)
    xt = features.reshape(count, ta, SIDE).transpose(1, 2, 0)
    hi = lax.reduce_precision(tiles[0, 0], 8, 7)
    lo = tiles[0, 0] - hi
    pack = jnp.concatenate([xt[0], hi.astype(BF), lo.astype(BF)], axis=1)
    weights = jnp.broadcast_to(weights_q.astype(BF), (NC, 16, count))
    scale = lax.all_to_all(weights, "col", 0, 0, tiled=True)[:, 0].astype(F32) / 64.0
    nxt, prev, far0, far1 = ring(pack, "x")
    line = jnp.stack([pack, nxt, jnp.concatenate([far0, far1]), prev])
    line = jnp.roll(line, row // 4, axis=0)
    first = gather_plane(line[:2])
    second = gather_plane(line[2:])
    rows = lax.all_to_all(xt.reshape(NC, -1, count), "col", 0, 0, tiled=True)
    prior = lax.all_to_all(tiles[0].reshape(NC, -1, SIDE), "col", 0, 0, tiled=True)
    inverse = factor_inverse(top_block(place, scale, first))
    near, lead, rest = own_rows(place, scale, rows, prior, first, second)
    back = solve_rows(inverse, near, lead, rest)
    back = lax.all_to_all(back, "col", 0, 0, tiled=True).astype(F32)
    back = back.transpose(1, 0, 2, 3).reshape(tcw, ta, SIDE, SIDE)
    row_tile = jnp.arange(ta, dtype=jnp.int32) * lax.axis_size("row") + row
    trailing = jnp.where(row_tile[:, None, None] < PW // SIDE, 0.0, tiles[1] + back[1])
    result = jnp.stack([back[0], trailing])
    return result.reshape(tcw, 1, ta, 1, SIDE, SIDE)


def solution(mesh):
    in_specs = (P(None, "col", None, "row", None, None), P("col", None, "row", None), P("col"))
    out_specs = P(None, "col", None, "row", None, None)
    return jax.shard_map(body, mesh=mesh, in_specs=in_specs, out_specs=out_specs, check_vma=False)
```

time: 855 us -> 282 us (0.33)
  other arithmetic: 289 us -> 5.9 us
  local copies, waits for them, and re-layouts: 171 us -> 17.1 us
  matrix products: 131 us -> 0 us
  Pallas kernels: 0 us -> 124 us
  waiting for transfers between devices: 177 us -> 59.5 us
  starting transfers between devices: 14 us -> 72.1 us
  blocking collectives: 49 us -> 0 us
  between operations: 19.1 us -> 0.35 us
    another operation x33 -> x5, other arithmetic: 258 us -> 2.49 us  [the longest x4 1.65 us: gather_plane(): mine = jnp.stack([u, nxt, jnp.concatenate([far0, far1]), prev])]
    all_gather x2 -> x0, waiting for transfers between devices: 151 us -> none  [body(): got = lax.all_gather(lax.all_gather(pack, 'col'), 'row')]
    pallas_call x0 -> x4, Pallas kernels: none -> 124 us  [the longest x1 67.9 us: factor_inverse(): pl.pallas_call(inverse_kernel, out_shape=jax.ShapeDtypeStruct((order, ord...]
    dot_general x5 -> x0, matrix products: 72.1 us -> none  [the longest x1 31.6 us: body(): lax.dot_general(window, weighted[:PW], (((1,), (1,)), ((), ())), preferre...]
    another operation x29 -> x0, matrix products: 58.8 us -> none  [the longest x15 35.8 us: factor_inverse(): jax.scipy.linalg.solve_triangular(factor, jnp.eye(block.shape[0], dtype=F...]
    transpose x3 -> x0, local copies, waits for them, and re-layouts: 55.9 us -> none  [the longest x2 46.8 us: body(): window = window.transpose(0, 2, 1, 3).reshape(nrow * side, ncol * count)]
    ppermute x0 -> x30, starting transfers between devices: none -> 50 us  [shift(): return lax.ppermute(x, ('row', 'col'), shift_pairs(kind, by))]
    all_gather x1 -> x0, blocking collectives: 49 us -> none  [body(): scale = lax.all_gather(weights_q, 'col').astype(F32) / 64.0]
  transfers between devices with their start and end apart: 5 -> 34, of which waited for: 3 -> 12; matrix products, arithmetic and copies ran while one was open for 66% -> 5% of each run, Pallas kernels for 0% -> 31%
where the time goes in v2:
time: 282 us; the launch traced here: 279 us
  Pallas kernels  124 us (44%)
  starting transfers between devices  72.1 us (26%)
  waiting for transfers between devices  59.5 us (21%)
  local copies, waits for them, and re-layouts  17.1 us (6%)
  other arithmetic  5.9 us (2%)
    pallas_call x1, Pallas kernels, factor_inverse(): pl.pallas_call(inverse_kernel, out_shape=jax.ShapeDtypeStruct((order, ord...  67.9 us
    ppermute x30, starting transfers between devices, shift(): return lax.ppermute(x, ('row', 'col'), shift_pairs(kind, by))  50 us
    ppermute x30, waiting for transfers between devices, shift(): return lax.ppermute(x, ('row', 'col'), shift_pairs(kind, by))  39.2 us
    pallas_call x1, Pallas kernels, own_rows(): pl.pallas_call(rows_kernel, out_shape=[jax.ShapeDtypeStruct((PW, PW), F32...  24.5 us
    pallas_call x1, Pallas kernels, top_block(): pl.pallas_call(top_kernel, out_shape=jax.ShapeDtypeStruct((PW, PW), F32),...  17.8 us
    all_to_all x1, waiting for transfers between devices, body(): back = lax.all_to_all(back, 'col', 0, 0, tiled=True).astype(F32)  13.4 us
    pallas_call x1, Pallas kernels, solve_rows(): pl.pallas_call(solve_kernel, out_shape=jax.ShapeDtypeStruct((NC, 2, own,...  13.4 us
    all_to_all x1, starting transfers between devices, body(): back = lax.all_to_all(back, 'col', 0, 0, tiled=True).astype(F32)  10.1 us
  transfers between devices with their start and end apart: 34, of which 12 were waited for; matrix products, arithmetic and copies ran while one was open for 5% of the time, Pallas kernels for 31%

profile of v2, /device:TPU:1, one launch (start us, length us, event | category | flops | bytes accessed | tf_op | source)
XLA Modules:
  0.0 278.6 jit_solution(624260707602426090)
XLA Ops:
  0.9 3.0 %copy.7 = bf16[512,16,1,128]{0,3,1,2:T(8,128)(2,1)S(1)} copy(bf16[512,16,1,128]{3,1,2,0:T(8,128)(2,1)} %param.4) | data formatting | bytes 4194304 | tf_op args[1]
  3.9 3.4 %collective-permute-start = (bf16[128,768]{1,0:T(8,128)(2,1)S(1)}, bf16[128,768]{1,0:T(8,128)(2,1)S(1)}, u32[]{:S(2)}, u32[]{:S(2)}) collective-permute-start(bf16[128,768]{1,0:T(8,128)(2,1)S(1)} %pad_maximum_fusion.2), channel_id=1, source_target_pairs={{0,96},{8,104},{2,98},{10,106},{4,100},{12,108},{6,102},{14,110},{... | collective-permute-start | bytes 589832 | tf_op jit(solution)/shard_map/ppermute | solution.py:61
  7.3 3.5 %collective-permute-done = bf16[128,768]{1,0:T(8,128)(2,1)S(1)} collective-permute-done((bf16[128,768]{1,0:T(8,128)(2,1)S(1)}, bf16[128,768]{1,0:T(8,128)(2,1)S(1)}, u32[]{:S(2)}, u32[]{:S(2)}) %collective-permute-start) | collective-permute-done | bytes 196640 | tf_op jit(solution)/shard_map/ppermute | solution.py:61
  10.9 3.5 %collective-permute-start.3 = (bf16[64,768]{1,0:T(8,128)(2,1)S(1)}, bf16[64,768]{1,0:T(8,128)(2,1)S(1)}, u32[]{:S(2)}, u32[]{:S(2)}) collective-permute-start(bf16[64,768]{1,0:T(8,128)(2,1)S(1)} %slice.88), channel_id=1, source_target_pairs={{0,96},{8,104},{2,98},{10,106},{4,100},{12,108},{6,102},{14,110},{... | collective-permute-start | bytes 294920 | tf_op jit(solution)/shard_map/ppermute | solution.py:61
  16.0 3.1 %collective-permute-done.2 = bf16[64,768]{1,0:T(8,128)(2,1)S(1)} collective-permute-done((bf16[64,768]{1,0:T(8,128)(2,1)S(1)}, bf16[64,768]{1,0:T(8,128)(2,1)S(1)}, u32[]{:S(2)}, u32[]{:S(2)}) %collective-permute-start.2) | collective-permute-done | bytes 98336 | tf_op jit(solution)/shard_map/ppermute | solution.py:61
  21.0 2.2 collective-permute-start.4
  23.2 2.7 collective-permute-start.17
  25.9 2.7 collective-permute-done.5
  28.8 2.7 collective-permute-start.7
  33.0 2.7 collective-permute-start.20
  43.0 7.2 %collective-permute-start.12 = (bf16[4,2,128,768]{3,2,1,0:T(8,128)(2,1)S(1)}, bf16[4,2,128,768]{3,2,1,0:T(8,128)(2,1)}, u32[]{:S(2)}, u32[]{:S(2)}) collective-permute-start(bf16[4,2,128,768]{3,2,1,0:T(8,128)(2,1)S(1)} %pad_maximum_fusion.refs_0_), channel_id=1, source_target_pairs={{0,8},{8,0},{2,10},{10,2},{4,12},{12,4},{6,14},{14,6},{1,9},{9,1},... | collective-permute-start | bytes 4718600 | tf_op jit(solution)/shard_map/ppermute | solution.py:61
  50.2 8.8 %collective-permute-done.9.refs_4_ = bf16[4,2,128,768]{3,2,1,0:T(8,128)(2,1)S(1)} collective-permute-done((bf16[4,2,128,768]{3,2,1,0:T(8,128)(2,1)S(1)}, bf16[4,2,128,768]{3,2,1,0:T(8,128)(2,1)S(1)}, u32[]{:S(2)}, u32[]{:S(2)}) %collective-permute-start.9) | collective-permute-done | bytes 1572896 | tf_op jit(solution)/shard_map/ppermute | solution.py:61
  62.1 2.7 collective-permute-start.11
  64.8 11.0 %collective-permute-done.22.refs_14_ = bf16[4,2,128,768]{3,2,1,0:T(8,128)(2,1)S(1)} collective-permute-done((bf16[4,2,128,768]{3,2,1,0:T(8,128)(2,1)}, bf16[4,2,128,768]{3,2,1,0:T(8,128)(2,1)S(1)}, u32[]{:S(2)}, u32[]{:S(2)}) %collective-permute-start.22) | collective-permute-done | bytes 1572896 | tf_op jit(solution)/shard_map/ppermute | solution.py:61
  75.8 2.8 %collective-permute-start.16 = (bf16[4,2,128,768]{3,2,1,0:T(8,128)(2,1)S(1)}, bf16[4,2,128,768]{3,2,1,0:T(8,128)(2,1)}, u32[]{:S(2)}, u32[]{:S(2)}) collective-permute-start(bf16[4,2,128,768]{3,2,1,0:T(8,128)(2,1)S(1)} %collective-permute-done.9.refs_4_), channel_id=1, source_target_pairs={{0,8},{8,0},{2,10},{10,2},{4,12},{12,4},{6,14},{14,6},{1,9},{9,1},... | collective-permute-start | bytes 4718600 | tf_op jit(solution)/shard_map/ppermute | solution.py:61
  79.3 3.4 %all-to-all-start = ((bf16[8,16,512]{2,1,0:T(8,128)(2,1)}), bf16[8,16,512]{2,1,0:T(8,128)(2,1)S(1)}, u32[]{:S(2)}, u32[]{:S(2)}) async-start(bf16[8,16,512]{2,1,0:T(8,128)(2,1)} %broadcast_in_dim.16), calls=%async_computation | async-start | bytes 262144 | tf_op jit(solution)/shard_map/all_to_all | solution.py:370
  82.7 2.3 slice.74
  85.0 3.2 %all-to-all-done = bf16[8,16,512]{2,1,0:T(8,128)(2,1)S(1)} async-done(((bf16[8,16,512]{2,1,0:T(8,128)(2,1)}), bf16[8,16,512]{2,1,0:T(8,128)(2,1)S(1)}, u32[]{:S(2)}, u32[]{:S(2)}) %all-to-all-start) | async-done | bytes 131104 | tf_op jit(solution)/shard_map/all_to_all | solution.py:370
  88.2 4.3 %all-to-all-start.2 = ((f32[8,256,128]{2,1,0:T(8,128)}), f32[8,256,128]{2,1,0:T(8,128)}, u32[]{:S(2)}, u32[]{:S(2)}) async-start(f32[8,256,128]{2,1,0:T(8,128)} %bitcast.60), calls=%async_computation.2 | async-start | bytes 2097152 | tf_op jit(solution)/shard_map/all_to_all | solution.py:377
  92.5 2.1 slice.95
  99.8 2.5 collective-permute-start.14
  102.4 3.6 %all-to-all-done.2.prior_ref = f32[8,256,128]{2,1,0:T(8,128)} async-done(((f32[8,256,128]{2,1,0:T(8,128)}), f32[8,256,128]{2,1,0:T(8,128)}, u32[]{:S(2)}, u32[]{:S(2)}) %all-to-all-start.2) | async-done | bytes 1048608 | tf_op jit(solution)/shard_map/all_to_all | solution.py:377
  106.0 4.4 %all-to-all-start.1 = ((bf16[8,256,512]{2,1,0:T(8,128)(2,1)}), bf16[8,256,512]{2,1,0:T(8,128)(2,1)}, u32[]{:S(2)}, u32[]{:S(2)}) async-start(bf16[8,256,512]{2,1,0:T(8,128)(2,1)} %bitcast.59), calls=%async_computation.1 | async-start | bytes 4194304 | tf_op jit(solution)/shard_map/all_to_all | solution.py:376
  110.4 2.5 collective-permute-done.23.refs_12_
  112.9 6.0 %collective-permute-start.25 = (bf16[4,2,128,768]{3,2,1,0:T(8,128)(2,1)}, bf16[4,2,128,768]{3,2,1,0:T(8,128)(2,1)}, u32[]{:S(2)}, u32[]{:S(2)}) collective-permute-start(bf16[4,2,128,768]{3,2,1,0:T(8,128)(2,1)} %pad_maximum_fusion.1.refs_10_), channel_id=1, source_target_pairs={{0,8},{8,0},{2,10},{10,2},{4,12},{12,4},{6,14},{14,6},{1,9},{9,1},... | collective-permute-start | bytes 4718600 | tf_op jit(solution)/shard_map/ppermute | solution.py:61
  119.7 4.6 %collective-permute-done.15.refs_8_ = bf16[2,2,128,768]{3,2,1,0:T(8,128)(2,1)S(1)} collective-permute-done((bf16[2,2,128,768]{3,2,1,0:T(8,128)(2,1)}, bf16[2,2,128,768]{3,2,1,0:T(8,128)(2,1)S(1)}, u32[]{:S(2)}, u32[]{:S(2)}) %collective-permute-start.15) | collective-permute-done | bytes 786464 | tf_op jit(solution)/shard_map/ppermute | solution.py:61
  126.8 17.8 %shard_map.37.s_ref = f32[1024,1024]{1,0:T(8,128)} custom-call(s32[3]{0:T(128)} %pad_add_fusion.pos_ref, f32[8,512]{1,0:T(8,128)} %multiply_bitcast_fusion.scale_ref, bf16[4,2,128,768]{3,2,1,0:T(8,128)(2,1)} %copy-done, bf16[4,2,128,768]{3,2,1,0:T(8,128)(2,1)} %collective-permute-done.8.refs_1_, bf16[2,2,128,768]{3,2,1,0:T(8,128)(2,1)} %collective-permute-done.10.refs_2_, ...), custom_call_target="tpu_custom_call" | custom-call | tf_op jit(solution)/shard_map/pallas_call | solution.py:146
  144.6 67.9 %shard_map.38.inv_ref = f32[1024,1024]{1,0:T(8,128)} custom-call(f32[1024,1024]{1,0:T(8,128)} %shard_map.37.s_ref), custom_call_target="tpu_custom_call" | custom-call | tf_op jit(solution)/shard_map/pallas_call | solution.py:312
  213.7 24.5 %shard_map.39 = (f32[1024,1024]{1,0:T(8,128)}, f32[256,1024]{1,0:T(8,128)}, f32[256,1024]{1,0:T(8,128)}) custom-call(s32[3]{0:T(128)} %pad_add_fusion.pos_ref, f32[8,512]{1,0:T(8,128)} %multiply_bitcast_fusion.scale_ref, bf16[8,256,512]{2,1,0:T(8,128)(2,1)} %all-to-all-done.1.rows_ref, f32[8,256,128]{2,1,0:T(8,128)} %all-to-all-done.2.prior_ref, ...), custom_call_target="tpu_custom_call" | custom-call | tf_op jit(solution)/shard_map/pallas_call | solution.py:206
  238.3 13.4 %shard_map.40 = bf16[8,2,256,128]{3,2,1,0:T(8,128)(2,1)} custom-call(f32[1024,1024]{1,0:T(8,128)} %shard_map.38.inv_ref, f32[1024,1024]{1,0:T(8,128)} %get-tuple-element.8.near_ref, f32[256,1024]{1,0:T(8,128)} %get-tuple-element.9.lead_ref, f32[256,1024]{1,0:T(8,128)} %get-tuple-element.10.rest_ref), custom_call_target="tpu_custom_call" | custom-call | tf_op jit(solution)/shard_map/pallas_call | solution.py:351
  251.6 10.1 %all-to-all-start.3 = ((bf16[8,2,256,128]{3,2,1,0:T(8,128)(2,1)}), bf16[8,2,256,128]{3,2,1,0:T(8,128)(2,1)S(1)}, u32[]{:S(2)}, u32[]{:S(2)}) async-start(bf16[8,2,256,128]{3,2,1,0:T(8,128)(2,1)} %shard_map.40), calls=%async_computation.3 | async-start | bytes 2097152 | tf_op jit(solution)/shard_map/all_to_all | solution.py:381
  261.7 13.4 %all-to-all-done.3 = bf16[8,2,256,128]{3,2,1,0:T(8,128)(2,1)S(1)} async-done(((bf16[8,2,256,128]{3,2,1,0:T(8,128)(2,1)}), bf16[8,2,256,128]{3,2,1,0:T(8,128)(2,1)S(1)}, u32[]{:S(2)}, u32[]{:S(2)}) %all-to-all-start.3) | async-done | bytes 1048608 | tf_op jit(solution)/shard_map/all_to_all | solution.py:381
  (96 shorter events, 30.2 us)
Async XLA Ops:
  3.9 6.9 %collective-permute-start = (bf16[128,768]{1,0:T(8,128)(2,1)S(1)}, bf16[128,768]{1,0:T(8,128)(2,1)S(1)}, u32[]{:S(2)}, u32[]{:S(2)}) collective-permute-start(bf16[128,768]{1,0:T(8,128)(2,1)S(1)} %pad_maximum_fusion.2), channel_id=1, source_target_pairs={{0,96},{8,104},{2,98},{10,106},{4,100},{12,108},{6,102},{14,110},{... | collective-permute-start | bytes 589832 | tf_op jit(solution)/shard_map/ppermute | solution.py:61
  7.3 7.1 %collective-permute-start.1 = (bf16[128,768]{1,0:T(8,128)(2,1)S(1)}, bf16[128,768]{1,0:T(8,128)(2,1)S(1)}, u32[]{:S(2)}, u32[]{:S(2)}) collective-permute-start(bf16[128,768]{1,0:T(8,128)(2,1)S(1)} %pad_maximum_fusion.2), channel_id=1, source_target_pairs={{0,32},{8,40},{2,34},{10,42},{4,36},{12,44},{6,38},{14,46},{1,33},... | collective-permute-start | bytes 589832 | tf_op jit(solution)/shard_map/ppermute | solution.py:61
  19.3 9.3 %collective-permute-start.5 = (bf16[2,128,768]{2,1,0:T(8,128)(2,1)S(1)}, bf16[2,128,768]{2,1,0:T(8,128)(2,1)S(1)}, u32[]{:S(2)}, u32[]{:S(2)}) collective-permute-start(bf16[2,128,768]{2,1,0:T(8,128)(2,1)S(1)} %get-tuple-element.16), channel_id=1, source_target_pairs={{0,1},{8,10},{2,3},{10,12},{4,5},{12,14},{6,7},{14,8},{1,16},{9,11... | collective-permute-start | bytes 1179656 | tf_op jit(solution)/shard_map/ppermute | solution.py:61
  21.0 7.7 %collective-permute-start.4 = (bf16[2,128,768]{2,1,0:T(8,128)(2,1)S(1)}, bf16[2,128,768]{2,1,0:T(8,128)(2,1)S(1)}, u32[]{:S(2)}, u32[]{:S(2)}) collective-permute-start(bf16[2,128,768]{2,1,0:T(8,128)(2,1)S(1)} %get-tuple-element.16), channel_id=1, source_target_pairs={{0,17},{8,14},{2,19},{10,8},{4,21},{12,10},{6,23},{14,12},{1,0},{9... | collective-permute-start | bytes 1179656 | tf_op jit(solution)/shard_map/ppermute | solution.py:61
  23.2 9.6 %collective-permute-start.18 = (bf16[2,128,768]{2,1,0:T(8,128)(2,1)S(1)}, bf16[2,128,768]{2,1,0:T(8,128)(2,1)S(1)}, u32[]{:S(2)}, u32[]{:S(2)}) collective-permute-start(bf16[2,128,768]{2,1,0:T(8,128)(2,1)S(1)} %get-tuple-element.15), channel_id=1, source_target_pairs={{0,1},{8,10},{2,3},{10,12},{4,5},{12,14},{6,7},{14,8},{1,16},{9,11... | collective-permute-start | bytes 1179656 | tf_op jit(solution)/shard_map/ppermute | solution.py:61
  23.2 9.7 %collective-permute-start.17 = (bf16[2,128,768]{2,1,0:T(8,128)(2,1)S(1)}, bf16[2,128,768]{2,1,0:T(8,128)(2,1)S(1)}, u32[]{:S(2)}, u32[]{:S(2)}) collective-permute-start(bf16[2,128,768]{2,1,0:T(8,128)(2,1)S(1)} %get-tuple-element.15), channel_id=1, source_target_pairs={{0,17},{8,14},{2,19},{10,8},{4,21},{12,10},{6,23},{14,12},{1,0},{9... | collective-permute-start | bytes 1179656 | tf_op jit(solution)/shard_map/ppermute | solution.py:61
  28.6 7.1 %collective-permute-start.6 = (bf16[1,128,768]{2,1,0:T(8,128)(2,1)S(1)}, bf16[1,128,768]{2,1,0:T(8,128)(2,1)S(1)}, u32[]{:S(2)}, u32[]{:S(2)}) collective-permute-start(bf16[1,128,768]{2,1,0:T(8,128)(2,1)S(1)} %slice.89), channel_id=1, source_target_pairs={{0,1},{8,10},{2,3},{10,12},{4,5},{12,14},{6,7},{14,8},{1,16},{9,11... | collective-permute-start | bytes 589832 | tf_op jit(solution)/shard_map/ppermute | solution.py:61
  28.8 6.9 %collective-permute-start.7 = (bf16[1,128,768]{2,1,0:T(8,128)(2,1)S(1)}, bf16[1,128,768]{2,1,0:T(8,128)(2,1)S(1)}, u32[]{:S(2)}, u32[]{:S(2)}) collective-permute-start(bf16[1,128,768]{2,1,0:T(8,128)(2,1)S(1)} %slice.90), channel_id=1, source_target_pairs={{0,17},{8,14},{2,19},{10,8},{4,21},{12,10},{6,23},{14,12},{1,0},{9... | collective-permute-start | bytes 589832 | tf_op jit(solution)/shard_map/ppermute | solution.py:61
  32.9 6.0 %collective-permute-start.19 = (bf16[1,128,768]{2,1,0:T(8,128)(2,1)S(1)}, bf16[1,128,768]{2,1,0:T(8,128)(2,1)S(1)}, u32[]{:S(2)}, u32[]{:S(2)}) collective-permute-start(bf16[1,128,768]{2,1,0:T(8,128)(2,1)S(1)} %slice.93), channel_id=1, source_target_pairs={{0,1},{8,10},{2,3},{10,12},{4,5},{12,14},{6,7},{14,8},{1,16},{9,11... | collective-permute-start | bytes 589832 | tf_op jit(solution)/shard_map/ppermute | solution.py:61
  33.0 5.9 %collective-permute-start.20 = (bf16[1,128,768]{2,1,0:T(8,128)(2,1)S(1)}, bf16[1,128,768]{2,1,0:T(8,128)(2,1)S(1)}, u32[]{:S(2)}, u32[]{:S(2)}) collective-permute-start(bf16[1,128,768]{2,1,0:T(8,128)(2,1)S(1)} %slice.94), channel_id=1, source_target_pairs={{0,17},{8,14},{2,19},{10,8},{4,21},{12,10},{6,23},{14,12},{1,0},{9... | collective-permute-start | bytes 589832 | tf_op jit(solution)/shard_map/ppermute | solution.py:61
  36.0 23.0 %collective-permute-start.9 = (bf16[4,2,128,768]{3,2,1,0:T(8,128)(2,1)S(1)}, bf16[4,2,128,768]{3,2,1,0:T(8,128)(2,1)S(1)}, u32[]{:S(2)}, u32[]{:S(2)}) collective-permute-start(bf16[4,2,128,768]{3,2,1,0:T(8,128)(2,1)S(1)} %pad_maximum_fusion.refs_0_), channel_id=1, source_target_pairs={{0,2},{8,9},{2,4},{10,11},{4,6},{12,13},{6,0},{14,15},{1,3},{9,24}... | collective-permute-start | bytes 4718600 | tf_op jit(solution)/shard_map/ppermute | solution.py:61
  37.0 23.0 %collective-permute-start.8 = (bf16[4,2,128,768]{3,2,1,0:T(8,128)(2,1)S(1)}, bf16[4,2,128,768]{3,2,1,0:T(8,128)(2,1)}, u32[]{:S(2)}, u32[]{:S(2)}) collective-permute-start(bf16[4,2,128,768]{3,2,1,0:T(8,128)(2,1)S(1)} %pad_maximum_fusion.refs_0_), channel_id=1, source_target_pairs={{0,6},{8,25},{2,0},{10,27},{4,2},{12,29},{6,4},{14,31},{1,7},{9,8}... | collective-permute-start | bytes 4718600 | tf_op jit(solution)/shard_map/ppermute | solution.py:61
  40.3 35.5 %collective-permute-start.22 = (bf16[4,2,128,768]{3,2,1,0:T(8,128)(2,1)}, bf16[4,2,128,768]{3,2,1,0:T(8,128)(2,1)S(1)}, u32[]{:S(2)}, u32[]{:S(2)}) collective-permute-start(bf16[4,2,128,768]{3,2,1,0:T(8,128)(2,1)} %pad_maximum_fusion.1.refs_10_), channel_id=1, source_target_pairs={{0,2},{8,9},{2,4},{10,11},{4,6},{12,13},{6,0},{14,15},{1,3},{9,24}... | collective-permute-start | bytes 4718600 | tf_op jit(solution)/shard_map/ppermute | solution.py:61
  41.1 53.6 %collective-permute-start.21 = (bf16[4,2,128,768]{3,2,1,0:T(8,128)(2,1)}, bf16[4,2,128,768]{3,2,1,0:T(8,128)(2,1)}, u32[]{:S(2)}, u32[]{:S(2)}) collective-permute-start(bf16[4,2,128,768]{3,2,1,0:T(8,128)(2,1)} %pad_maximum_fusion.1.refs_10_), channel_id=1, source_target_pairs={{0,6},{8,25},{2,0},{10,27},{4,2},{12,29},{6,4},{14,31},{1,7},{9,8}... | collective-permute-start | bytes 4718600 | tf_op jit(solution)/shard_map/ppermute | solution.py:61
  43.0 55.1 %collective-permute-start.12 = (bf16[4,2,128,768]{3,2,1,0:T(8,128)(2,1)S(1)}, bf16[4,2,128,768]{3,2,1,0:T(8,128)(2,1)}, u32[]{:S(2)}, u32[]{:S(2)}) collective-permute-start(bf16[4,2,128,768]{3,2,1,0:T(8,128)(2,1)S(1)} %pad_maximum_fusion.refs_0_), channel_id=1, source_target_pairs={{0,8},{8,0},{2,10},{10,2},{4,12},{12,4},{6,14},{14,6},{1,9},{9,1},... | collective-permute-start | bytes 4718600 | tf_op jit(solution)/shard_map/ppermute | solution.py:61
  60.0 39.8 %collective-permute-start.10 = (bf16[2,2,128,768]{3,2,1,0:T(8,128)(2,1)}, bf16[2,2,128,768]{3,2,1,0:T(8,128)(2,1)}, u32[]{:S(2)}, u32[]{:S(2)}) collective-permute-start(bf16[2,2,128,768]{3,2,1,0:T(8,128)(2,1)} %slice.91), channel_id=1, source_target_pairs={{0,2},{8,9},{2,4},{10,11},{4,6},{12,13},{6,0},{14,15},{1,3},{9,24}... | collective-permute-start | bytes 2359304 | tf_op jit(solution)/shard_map/ppermute | solution.py:61
  62.1 40.2 %collective-permute-start.11 = (bf16[2,2,128,768]{3,2,1,0:T(8,128)(2,1)}, bf16[2,2,128,768]{3,2,1,0:T(8,128)(2,1)}, u32[]{:S(2)}, u32[]{:S(2)}) collective-permute-start(bf16[2,2,128,768]{3,2,1,0:T(8,128)(2,1)} %slice.92), channel_id=1, source_target_pairs={{0,6},{8,25},{2,0},{10,27},{4,2},{12,29},{6,4},{14,31},{1,7},{9,8}... | collective-permute-start | bytes 2359304 | tf_op jit(solution)/shard_map/ppermute | solution.py:61
  75.8 43.6 %collective-permute-start.16 = (bf16[4,2,128,768]{3,2,1,0:T(8,128)(2,1)S(1)}, bf16[4,2,128,768]{3,2,1,0:T(8,128)(2,1)}, u32[]{:S(2)}, u32[]{:S(2)}) collective-permute-start(bf16[4,2,128,768]{3,2,1,0:T(8,128)(2,1)S(1)} %collective-permute-done.9.refs_4_), channel_id=1, source_target_pairs={{0,8},{8,0},{2,10},{10,2},{4,12},{12,4},{6,14},{14,6},{1,9},{9,1},... | collective-permute-start | bytes 4718600 | tf_op jit(solution)/shard_map/ppermute | solution.py:61
  79.3 8.9 %all-to-all-start = ((bf16[8,16,512]{2,1,0:T(8,128)(2,1)}), bf16[8,16,512]{2,1,0:T(8,128)(2,1)S(1)}, u32[]{:S(2)}, u32[]{:S(2)}) async-start(bf16[8,16,512]{2,1,0:T(8,128)(2,1)} %broadcast_in_dim.16), calls=%async_computation | async-start | bytes 262144 | tf_op jit(solution)/shard_map/all_to_all | solution.py:370
  88.2 17.8 %all-to-all-start.2 = ((f32[8,256,128]{2,1,0:T(8,128)}), f32[8,256,128]{2,1,0:T(8,128)}, u32[]{:S(2)}, u32[]{:S(2)}) async-start(f32[8,256,128]{2,1,0:T(8,128)} %bitcast.60), calls=%async_computation.2 | async-start | bytes 2097152 | tf_op jit(solution)/shard_map/all_to_all | solution.py:377
  94.6 18.3 %collective-permute-start.23 = (bf16[2,2,128,768]{3,2,1,0:T(8,128)(2,1)}, bf16[2,2,128,768]{3,2,1,0:T(8,128)(2,1)}, u32[]{:S(2)}, u32[]{:S(2)}) collective-permute-start(bf16[2,2,128,768]{3,2,1,0:T(8,128)(2,1)} %slice.95), channel_id=1, source_target_pairs={{0,2},{8,9},{2,4},{10,11},{4,6},{12,13},{6,0},{14,15},{1,3},{9,24}... | collective-permute-start | bytes 2359304 | tf_op jit(solution)/shard_map/ppermute | solution.py:61
  98.1 20.8 %collective-permute-start.24 = (bf16[2,2,128,768]{3,2,1,0:T(8,128)(2,1)}, bf16[2,2,128,768]{3,2,1,0:T(8,128)(2,1)}, u32[]{:S(2)}, u32[]{:S(2)}) collective-permute-start(bf16[2,2,128,768]{3,2,1,0:T(8,128)(2,1)} %slice.96), channel_id=1, source_target_pairs={{0,6},{8,25},{2,0},{10,27},{4,2},{12,29},{6,4},{14,31},{1,7},{9,8}... | collective-permute-start | bytes 2359304 | tf_op jit(solution)/shard_map/ppermute | solution.py:61
  99.8 19.1 %collective-permute-start.14 = (bf16[2,2,128,768]{3,2,1,0:T(8,128)(2,1)}, bf16[2,2,128,768]{3,2,1,0:T(8,128)(2,1)}, u32[]{:S(2)}, u32[]{:S(2)}) collective-permute-start(bf16[2,2,128,768]{3,2,1,0:T(8,128)(2,1)} %collective-permute-done.10.refs_2_), channel_id=1, source_target_pairs={{0,8},{8,0},{2,10},{10,2},{4,12},{12,4},{6,14},{14,6},{1,9},{9,1},... | collective-permute-start | bytes 2359304 | tf_op jit(solution)/shard_map/ppermute | solution.py:61
  102.3 22.1 %collective-permute-start.13 = (bf16[4,2,128,768]{3,2,1,0:T(8,128)(2,1)}, bf16[4,2,128,768]{3,2,1,0:T(8,128)(2,1)S(1)}, u32[]{:S(2)}, u32[]{:S(2)}) collective-permute-start(bf16[4,2,128,768]{3,2,1,0:T(8,128)(2,1)} %collective-permute-done.8.refs_1_), channel_id=1, source_target_pairs={{0,8},{8,0},{2,10},{10,2},{4,12},{12,4},{6,14},{14,6},{1,9},{9,1},... | collective-permute-start | bytes 4718600 | tf_op jit(solution)/shard_map/ppermute | solution.py:61
  106.0 106.5 %all-to-all-start.1 = ((bf16[8,256,512]{2,1,0:T(8,128)(2,1)}), bf16[8,256,512]{2,1,0:T(8,128)(2,1)}, u32[]{:S(2)}, u32[]{:S(2)}) async-start(bf16[8,256,512]{2,1,0:T(8,128)(2,1)} %bitcast.59), calls=%async_computation.1 | async-start | bytes 4194304 | tf_op jit(solution)/shard_map/all_to_all | solution.py:376
  112.9 99.6 %collective-permute-start.25 = (bf16[4,2,128,768]{3,2,1,0:T(8,128)(2,1)}, bf16[4,2,128,768]{3,2,1,0:T(8,128)(2,1)}, u32[]{:S(2)}, u32[]{:S(2)}) collective-permute-start(bf16[4,2,128,768]{3,2,1,0:T(8,128)(2,1)} %pad_maximum_fusion.1.refs_10_), channel_id=1, source_target_pairs={{0,8},{8,0},{2,10},{10,2},{4,12},{12,4},{6,14},{14,6},{1,9},{9,1},... | collective-permute-start | bytes 4718600 | tf_op jit(solution)/shard_map/ppermute | solution.py:61
  118.9 5.4 %collective-permute-start.15 = (bf16[2,2,128,768]{3,2,1,0:T(8,128)(2,1)}, bf16[2,2,128,768]{3,2,1,0:T(8,128)(2,1)S(1)}, u32[]{:S(2)}, u32[]{:S(2)}) collective-permute-start(bf16[2,2,128,768]{3,2,1,0:T(8,128)(2,1)} %collective-permute-done.11.refs_3_), channel_id=1, source_target_pairs={{0,8},{8,0},{2,10},{10,2},{4,12},{12,4},{6,14},{14,6},{1,9},{9,1},... | collective-permute-start | bytes 2359304 | tf_op jit(solution)/shard_map/ppermute | solution.py:61
  118.9 93.6 %collective-permute-start.29 = (bf16[4,2,128,768]{3,2,1,0:T(8,128)(2,1)}, bf16[4,2,128,768]{3,2,1,0:T(8,128)(2,1)}, u32[]{:S(2)}, u32[]{:S(2)}) collective-permute-start(bf16[4,2,128,768]{3,2,1,0:T(8,128)(2,1)} %copy-done.4), channel_id=1, source_target_pairs={{0,8},{8,0},{2,10},{10,2},{4,12},{12,4},{6,14},{14,6},{1,9},{9,1},... | collective-permute-start | bytes 4718600 | tf_op jit(solution)/shard_map/ppermute | solution.py:61
  119.4 93.1 %collective-permute-start.26 = (bf16[4,2,128,768]{3,2,1,0:T(8,128)(2,1)}, bf16[4,2,128,768]{3,2,1,0:T(8,128)(2,1)S(1)}, u32[]{:S(2)}, u32[]{:S(2)}) collective-permute-start(bf16[4,2,128,768]{3,2,1,0:T(8,128)(2,1)} %collective-permute-done.21.refs_11_), channel_id=1, source_target_pairs={{0,8},{8,0},{2,10},{10,2},{4,12},{12,4},{6,14},{14,6},{1,9},{9,1},... | collective-permute-start | bytes 4718600 | tf_op jit(solution)/shard_map/ppermute | solution.py:61
  124.3 88.3 %collective-permute-start.27 = (bf16[2,2,128,768]{3,2,1,0:T(8,128)(2,1)}, bf16[2,2,128,768]{3,2,1,0:T(8,128)(2,1)}, u32[]{:S(2)}, u32[]{:S(2)}) collective-permute-start(bf16[2,2,128,768]{3,2,1,0:T(8,128)(2,1)} %collective-permute-done.23.refs_12_), channel_id=1, source_target_pairs={{0,8},{8,0},{2,10},{10,2},{4,12},{12,4},{6,14},{14,6},{1,9},{9,1},... | collective-permute-start | bytes 2359304 | tf_op jit(solution)/shard_map/ppermute | solution.py:61
  125.2 87.4 %collective-permute-start.28 = (bf16[2,2,128,768]{3,2,1,0:T(8,128)(2,1)}, bf16[2,2,128,768]{3,2,1,0:T(8,128)(2,1)}, u32[]{:S(2)}, u32[]{:S(2)}) collective-permute-start(bf16[2,2,128,768]{3,2,1,0:T(8,128)(2,1)} %collective-permute-done.24.refs_13_), channel_id=1, source_target_pairs={{0,8},{8,0},{2,10},{10,2},{4,12},{12,4},{6,14},{14,6},{1,9},{9,1},... | collective-permute-start | bytes 2359304 | tf_op jit(solution)/shard_map/ppermute | solution.py:61
  251.6 23.5 %all-to-all-start.3 = ((bf16[8,2,256,128]{3,2,1,0:T(8,128)(2,1)}), bf16[8,2,256,128]{3,2,1,0:T(8,128)(2,1)S(1)}, u32[]{:S(2)}, u32[]{:S(2)}) async-start(bf16[8,2,256,128]{3,2,1,0:T(8,128)(2,1)} %shard_map.40), calls=%async_computation.3 | async-start | bytes 2097152 | tf_op jit(solution)/shard_map/all_to_all | solution.py:381
  (11 other events, 95.5 us)
